TPU v7x, 128 devices: a whole 4x4x4 slice. The times are simulated.
128 devices in a mesh: state: 32 (over z, x, core), rank: 4 (over y).
Axes of the slice: x: 4, y: 4, z: 4, core: 2. Of those that a mesh axis runs over, the one named last changes fastest.
Arguments:
- token_ids: int32 [3, 128], replicated, may hold values from 0 to 9999
- word_emb: bfloat16 [10000, 128], replicated, may hold values from -6 to 6
- state_emb: bfloat16 [131072, 128], P('state'), may hold values from -3 to 3
- log_norm: float32 [131072], P('state'), may hold values from -0.5 to 1
- beta_last: bfloat16 [131072, 128], P('state'), may hold values from 0.19921875 to 5
- forward_marg: bfloat16 [131072, 384], P('state'), may hold values from 0.049804688 to 2
- trans_left: bfloat16 [131072, 2048], P('state', 'rank'), as said below
- trans_right: bfloat16 [131072, 2048], P('state', 'rank'), as said below
Outputs:
- beta_first: bfloat16 [131072, 128], P('state')
- grad_left: bfloat16 [131072, 2048], P('state', 'rank')
- grad_right: bfloat16 [131072, 2048], P('state', 'rank')
Inputs may be any that keep to these rules, and one draw needn't show every extreme that they name: `trans_left`: positive entries. `trans_right`: positive entries.
All inputs are finite; a program needn't handle non-finite values.
Results may differ from a plain program's by a relative error of at most 0.009.
Values may be sent and summed in bfloat16 or wider, within the bound.
A program may use at most 128 MiB of HBM per device.

v0:
```python
import jax
import jax.numpy as jnp
from jax import lax
from jax.sharding import PartitionSpec as P


def on_device(
    token_ids, word_emb, state_emb, log_norm, beta_last, forward_marg, trans_left, trans_right
):
    states_all = lax.axis_size("state") * state_emb.shape[0]
    steps = token_ids.shape[0]
    batch = beta_last.shape[1]
    local_columns = jnp.sum(trans_left, axis=0, dtype=jnp.float32)
    fwd_part = lax.dot_general(
        forward_marg, trans_left, (((0,), (0,)), ((), ())), preferred_element_type=jnp.float32
    )
    fwd_proj = (lax.psum(fwd_part, "state") / states_all).astype(jnp.bfloat16)
    beta = beta_last
    weighted_list = []
    proj_list = []
    for step in reversed(range(steps)):
        words = jnp.take(word_emb, token_ids[step], axis=0)
        logits = jnp.dot(state_emb, words.T, preferred_element_type=jnp.float32)
        emit = jnp.exp(logits - log_norm[:, None])
        weighted = (emit * beta.astype(jnp.float32)).astype(jnp.bfloat16)
        proj_part = lax.dot_general(
            weighted, trans_right, (((0,), (0,)), ((), ())), preferred_element_type=jnp.float32
        )
        projb = lax.psum(proj_part, "state").astype(jnp.bfloat16)
        total = lax.psum(jnp.dot(projb.astype(jnp.float32), local_columns), ("state", "rank"))
        mass = total / states_all
        raw_part = lax.dot_general(
            trans_left, projb, (((1,), (1,)), ((), ())), preferred_element_type=jnp.float32
        )
        raw = lax.psum(raw_part, "rank")
        beta = (raw / mass[None, :]).astype(jnp.bfloat16)
        weighted_list.insert(0, weighted)
        proj_list.insert(0, projb)
    weighted_all = jnp.concatenate(weighted_list, axis=1)
    proj_all = jnp.concatenate(proj_list, axis=0)
    count = steps * batch
    grad_left = (
        jnp.dot(forward_marg, proj_all, preferred_element_type=jnp.float32) / count
    ).astype(jnp.bfloat16)
    grad_right = (
        jnp.dot(weighted_all, fwd_proj, preferred_element_type=jnp.float32) / count
    ).astype(jnp.bfloat16)
    return (beta, grad_left, grad_right)


def solution(mesh):
    placed = (
        P(),
        P(),
        P("state", None),
        P("state"),
        P("state", None),
        P("state", None),
        P("state", "rank"),
        P("state", "rank"),
    )
    return jax.shard_map(
        on_device,
        mesh=mesh,
        in_specs=placed,
        out_specs=(P("state", None), P("state", "rank"), P("state", "rank")),
        check_vma=False,
    )
```

profile of v0, /device:TPU:1, one launch (start us, length us, event | category | flops | bytes accessed | tf_op | source)
XLA Modules:
  0.0 664.9 jit_solution(3494271662389963587)
XLA Ops:
  7.2 0.9 compare_and_fusion.2
  8.1 2.3 copy.11
  10.4 2.7 gather_fusion.2
  13.1 2.1 fusion.12
  15.3 1.0 copy-done.3
  16.2 3.0 fusion.39
  19.2 126.7 %all-reduce.15 = bf16[128,512]{1,0:T(8,128)(2,1)S(1)} all-reduce(f32[128,512]{1,0:T(8,128)S(1)} %fusion.39), channel_id=1, replica_groups=mesh['state'=32,'rank'=4] {'state'}, use_global_device_ids=true, to_apply=%region_0.2 | all-reduce | flops 65536 | bytes 393216 | tf_op jit(solution)/shard_map/psum | solution.py:29
  145.9 5.0 convolution_bitcast_fusion.2
  151.0 2.7 gather_fusion.1
  153.7 2.8 convert_reduce_fusion
  156.5 0.1 convolution_bitcast_fusion.5
  156.6 69.2 %psum.72 = f32[128]{0:T(128)S(1)} all-reduce(f32[128]{0:T(128)S(1)} %convolution_bitcast_fusion.5), channel_id=1, replica_groups=mesh['state'=32,'rank'=4] {'state','rank'}, use_global_device_ids=true, to_apply=%region_3.5 | all-reduce | flops 128 | bytes 1024 | tf_op jit(solution)/shard_map/psum | solution.py:30
  225.8 2.6 fusion.11
  228.5 1.0 copy-done.4
  229.5 1.4 fusion.40
  230.9 122.8 %all-reduce.16 = bf16[128,512]{1,0:T(8,128)(2,1)S(1)} all-reduce(f32[128,512]{1,0:T(8,128)} %fusion.40), channel_id=1, replica_groups=mesh['state'=32,'rank'=4] {'state'}, use_global_device_ids=true, to_apply=%region_4.6 | all-reduce | flops 65536 | bytes 393216 | tf_op jit(solution)/shard_map/psum | solution.py:29
  353.7 5.0 convolution_bitcast_fusion.1
  358.8 4.9 fusion.42
  363.7 2.7 gather_fusion
  366.4 0.1 convolution_bitcast_fusion.4
  366.6 68.3 %psum.75 = f32[128]{0:T(128)S(1)} all-reduce(f32[128]{0:T(128)S(1)} %convolution_bitcast_fusion.4), channel_id=1, replica_groups=mesh['state'=32,'rank'=4] {'state','rank'}, use_global_device_ids=true, to_apply=%region_6.8 | all-reduce | flops 128 | bytes 1024 | tf_op jit(solution)/shard_map/psum | solution.py:30
  434.9 2.6 fusion.10
  437.6 1.0 copy-done.5
  438.6 1.4 fusion.41
  440.0 123.2 %all-reduce.17 = bf16[128,512]{1,0:T(8,128)(2,1)S(1)} all-reduce(f32[128,512]{1,0:T(8,128)} %fusion.41), channel_id=1, replica_groups=mesh['state'=32,'rank'=4] {'state'}, use_global_device_ids=true, to_apply=%region_7.9 | all-reduce | flops 65536 | bytes 393216 | tf_op jit(solution)/shard_map/psum | solution.py:29
  563.1 5.0 convolution_bitcast_fusion
  568.1 4.4 fusion
  572.5 6.4 copy.13
  579.1 67.8 %psum.78 = f32[128]{0:T(128)S(1)} all-reduce(f32[128]{0:T(128)S(1)} %convolution_bitcast_fusion.3), channel_id=1, replica_groups=mesh['state'=32,'rank'=4] {'state','rank'}, use_global_device_ids=true, to_apply=%region_9.11 | all-reduce | flops 128 | bytes 1024 | tf_op jit(solution)/shard_map/psum | solution.py:30
  646.8 6.5 multiply_convert_fusion
  653.3 2.8 divide_convert_fusion
  656.1 2.3 copy.12
  (30 shorter events, 0.4 us)
Async XLA Ops:
  7.2 351.6 %copy-start = (bf16[4096,384]{1,0:T(8,128)(2,1)S(1)}, bf16[4096,384]{1,0:T(8,128)(2,1)}, u32[]{:S(2)}) copy-start(bf16[4096,384]{1,0:T(8,128)(2,1)} %param.15) | copy-start | bytes 9437188
  7.2 218.7 %all-reduce.8.cloned.1.call-start = ((), (), s32[]{:S(2)}) async-start(), calls=%async_computation | async-start | bytes 4194304 | tf_op jit(solution)/shard_map/psum | solution.py:35
  15.3 1.0 copy-start.3
  150.9 74.9 %copy-start.6 = (f32[4096]{0:T(1024)S(1)}, f32[4096]{0:T(1024)}, u32[]{:S(2)}) copy-start(f32[4096]{0:T(1024)} %param.13) | copy-start | bytes 49156
  150.9 284.0 %all-reduce.10.cloned.1.call-start = ((), (), s32[]{:S(2)}) async-start(), calls=%async_computation.1 | async-start | bytes 4194304 | tf_op jit(solution)/shard_map/psum | solution.py:35
  225.8 3.6 copy-start.1
  228.5 1.0 copy-start.4
  358.7 288.1 %all-reduce.14.cloned.1.call-start = ((), (), s32[]{:S(2)}) async-start(), calls=%async_computation.3 | async-start | bytes 1572864 | tf_op jit(solution)/shard_map/psum | solution.py:17
  363.7 289.7 %all-reduce.12.cloned.1.call-start = ((), (), s32[]{:S(2)}) async-start(), calls=%async_computation.2 | async-start | bytes 4194304 | tf_op jit(solution)/shard_map/psum | solution.py:35
  434.9 3.7 copy-start.2
  437.6 1.0 copy-start.5
Sparse Core Ops, SparseCore 0:
  151.0 61.0 all-reduce.7
  358.8 59.1 all-reduce.9
  421.2 103.5 all-reduce.13
  568.2 58.8 all-reduce.11
where the time goes:
time: 666 us; the launch traced here: 665 us
  blocking collectives  578 us (87%)
  matrix products  44.3 us (7%)
  local copies, waits for them, and re-layouts  22 us (3%)
  between operations  13.9 us (2%)
    psum x3, blocking collectives, on_device(): projb = lax.psum(proj_part, 'state').astype(jnp.bfloat16)  373 us
    psum x3, blocking collectives, on_device(): lax.psum(jnp.dot(projb.astype(jnp.float32), local_columns), ('state', 'ra...  205 us
    dot_general x3, matrix products, on_device(): lax.dot_general(trans_left, projb, (((1,), (1,)), ((), ())), preferred_el...  14.9 us
    unnamed x17, local copies, waits for them, and re-layouts  13.9 us
  transfers between devices with their start and end apart: 4, of which 0 were waited for; matrix products, arithmetic and copies ran while one was open for 6% of the time, Pallas kernels for 0%

commit v1 on v0

v1 whole, which is shorter than its diff:
```python
import functools

import jax
import jax.numpy as jnp
from jax import lax
from jax.experimental import pallas as pl
from jax.experimental.pallas import tpu as pltpu
from jax.sharding import PartitionSpec as P

MESH = pl.DeviceIdType.MESH
F32 = jnp.float32
BF16 = jnp.bfloat16
GROUP = 8
RANKS = 4
BLOCKS = 2 * RANKS
HALVES = 2
STEPS = 3


def nn(a, b):
    return lax.dot_general(a, b, (((1,), (0,)), ((), ())), preferred_element_type=F32)


def nt(a, b):
    return lax.dot_general(a, b, (((1,), (1,)), ((), ())), preferred_element_type=F32)


def recursion(
    states_all, zs,
    ids, word_emb, semb, ln, beta, fm, left, right,
    wn_o, pb_o, fw_o, bt_o,
    ids_v, emb_v, semb_v, ln_v, beta_v, fm_v, u_v, v_v,
    words, w, wn, emit, acc, keep, csm, pb,
    sb1, rb1, rb2, pj, fs1, fr1, fr2, fj, cs, cr1, cr2,
    rs_s, rs_r, ms, mr,
    load, store, s1s, s1r, s2s, s2r, s3s, s3r, f1s, f1r, f2s, f2r, f3s, f3r, cs_s, cs_r,
    rss, rsr, ags, agr, mss, msr,
):
    state = lax.axis_index("state")
    y = lax.axis_index("rank")
    g = lax.rem(state, GROUP)
    z = state // GROUP
    yp, yo, ym = lax.rem(y + 1, RANKS), lax.rem(y + 2, RANKS), lax.rem(y + 3, RANKS)
    vocab, hidden = word_emb.shape
    padded = emb_v.shape[0]
    local, ranks = left.shape
    blk = local // BLOCKS
    hb = w.shape[3]
    batch = HALVES * hb
    half_ranks = ranks // 2

    loads = [
        (ids, ids_v), (word_emb, emb_v.at[pl.ds(0, vocab)]), (semb, semb_v), (ln, ln_v), (beta, beta_v),
        (right, v_v), (left, u_v), (fm, fm_v),
    ]
    loads = [pltpu.make_async_copy(src, dst, load.at[k]) for k, (src, dst) in enumerate(loads)]
    for copy in loads:
        copy.start()
    ids_l, emb_l, semb_l, ln_l, beta_l, v_l, u_l, fm_l = loads

    def group_peer(d):
        p = lax.rem(g + d, GROUP)
        return p, (z * GROUP + p, y)

    def z_peer(d):
        return (lax.rem(z + d, zs) * GROUP + g, y)

    barrier = pltpu.get_barrier_semaphore()
    greeted = [group_peer(d)[1] for d in range(1, GROUP)] + [z_peer(d) for d in range(1, zs)]
    greeted += [(state, other) for other in (yp, yo, ym)]
    for who in greeted:
        pl.semaphore_signal(barrier, inc=1, device_id=who, device_id_type=MESH)

    def send(src, dst, send_sem, recv_sem, who):
        pltpu.make_async_remote_copy(
            src_ref=src, dst_ref=dst, send_sem=send_sem, recv_sem=recv_sem, device_id=who, device_id_type=MESH
        ).start()

    def await_bytes(ref, sem):
        pltpu.make_async_copy(ref, ref, sem).wait()

    def rows(ref, j):
        return ref[pl.ds(pl.multiple_of(j * blk, blk), blk), :]

    emb_v[pl.ds(vocab, padded - vocab), :] = jnp.zeros((padded - vocab, hidden), BF16)
    chunk = 1024

    def find_words(t, column):
        def one(c, total):
            lane = lax.broadcasted_iota(jnp.int32, (batch, chunk), 1) + c * chunk
            hot = jnp.where(lane.astype(F32) == column, 1.0, 0.0).astype(BF16)
            return total + nn(hot, emb_v[pl.ds(pl.multiple_of(c * chunk, chunk), chunk), :])

        total = lax.fori_loop(0, padded // chunk, one, jnp.zeros((batch, hidden), F32))
        words[t] = total.astype(BF16)

    ids_l.wait()
    id_rows = jnp.concatenate([ids_v[...].astype(F32), jnp.zeros((8 - STEPS, batch), F32)], axis=0)
    id_cols = id_rows.T
    emb_l.wait()
    find_words(STEPS - 1, id_cols[:, STEPS - 1:STEPS])

    semb_l.wait()
    ln_l.wait()
    beta_l.wait()
    v_l.wait()
    eye = jnp.where(
        lax.broadcasted_iota(jnp.int32, (batch, batch), 0) == lax.broadcasted_iota(jnp.int32, (batch, batch), 1), 1.0, 0.0
    ).astype(BF16)

    def first(j, total):
        logits = nt(words[STEPS - 1], rows(semb_v, j))
        em = jnp.exp(logits - ln_v[j])
        wt = (em * nt(eye, rows(beta_v, j))).astype(BF16)
        for h in range(HALVES):
            w[0, h, j] = wt[h * hb:(h + 1) * hb]
        return total + nn(wt, rows(v_v, j))

    total = lax.fori_loop(0, BLOCKS, first, jnp.zeros((batch, ranks), F32))
    for h in range(HALVES):
        acc[h] = total[h * hb:(h + 1) * hb]

    pl.semaphore_wait(barrier, len(greeted))

    def sum1(i, h):
        part = acc[h].astype(BF16)
        for p in range(GROUP):
            r, c = 16 * (p % 4), half_ranks * (p // 4)
            sb1[i, h, p] = part[r:r + 16, c:c + half_ranks]
        for d in range(1, GROUP):
            p, who = group_peer(d)
            send(sb1.at[i, h, p], rb1.at[i, h, d - 1], s1s.at[i, h], s1r.at[i, h], who)

    def sum2(i, h):
        await_bytes(rb1.at[i, h], s1r.at[i, h])
        total = sb1[i, h, g].astype(F32)
        for d in range(GROUP - 1):
            total += rb1[i, h, d].astype(F32)
        rb2[i, h, z] = total.astype(BF16)
        for d in range(1, zs):
            send(rb2.at[i, h, z], rb2.at[i, h, z], s2s.at[i, h], s2r.at[i, h], z_peer(d))

    def sum3(i, h):
        await_bytes(rb2.at[i, h, pl.ds(0, zs - 1)], s2r.at[i, h])
        total = rb2[i, h, 0].astype(F32)
        for d in range(1, zs):
            total += rb2[i, h, d].astype(F32)
        pj[i, h, g] = total.astype(BF16)
        for d in range(1, GROUP):
            send(pj.at[i, h, g], pj.at[i, h, g], s3s.at[i, h], s3r.at[i, h], group_peer(d)[1])

    def fwd1(i):
        t = STEPS - 1 - i

        def one(j, total):
            cols = fm_v[pl.ds(pl.multiple_of(j * blk, blk), blk), pl.ds(pl.multiple_of(t * batch, batch), batch)]
            return total + nn(cols.T, rows(u_v, j))

        total = lax.fori_loop(0, BLOCKS, one, jnp.zeros((batch, ranks), F32))
        for p in range(GROUP):
            fs1[i, p] = total[16 * p:16 * p + 16].astype(BF16)
        for d in range(1, GROUP):
            p, who = group_peer(d)
            send(fs1.at[i, p], fr1.at[i, d - 1], f1s.at[i], f1r.at[i], who)

    def fwd2(i):
        await_bytes(fr1.at[i], f1r.at[i])
        total = fs1[i, g].astype(F32)
        for d in range(GROUP - 1):
            total += fr1[i, d].astype(F32)
        fr2[i, z] = total.astype(BF16)
        for d in range(1, zs):
            send(fr2.at[i, z], fr2.at[i, z], f2s.at[i], f2r.at[i], z_peer(d))

    def fwd3(i):
        await_bytes(fr2.at[i, pl.ds(0, zs - 1)], f2r.at[i])
        total = fr2[i, 0].astype(F32)
        for d in range(1, zs):
            total += fr2[i, d].astype(F32)
        fj[i, g] = (total / states_all).astype(BF16)
        for d in range(1, GROUP):
            send(fj.at[i, g], fj.at[i, g], f3s.at[i], f3r.at[i], group_peer(d)[1])

    tiles = ranks // 128

    def columns1():
        def one(j, total):
            return total + nn(jnp.ones((16, blk), BF16), rows(u_v, j))

        total = lax.fori_loop(0, BLOCKS, one, jnp.zeros((16, ranks), F32))
        cs[...] = jnp.zeros_like(cs)
        for c in range(tiles):
            cs[0, c:c + 1, :] = total[0:1, 128 * c:128 * c + 128]
        for d in range(1, GROUP):
            send(cs.at[0], cr1.at[d - 1], cs_s.at[0], cs_r.at[0], group_peer(d)[1])

    def columns2():
        await_bytes(cr1, cs_r.at[0])
        total = cs[0]
        for d in range(GROUP - 1):
            total += cr1[d]
        cs[1] = total
        for d in range(1, zs):
            send(cs.at[1], cr2.at[d - 1], cs_s.at[1], cs_r.at[1], z_peer(d))

    def columns3():
        await_bytes(cr2, cs_r.at[1])
        total = cs[1]
        for d in range(zs - 1):
            total += cr2[d]
        line = jnp.concatenate([total[c:c + 1] for c in range(tiles)], axis=1)
        high = line.astype(BF16)
        rest = line - high.astype(F32)
        mid = rest.astype(BF16)
        low = (rest - mid.astype(F32)).astype(BF16)
        parts = [x.astype(F32) for x in (high, mid, low)] + [jnp.zeros((13, ranks), F32)]
        csm[...] = jnp.concatenate(parts, axis=0).astype(BF16)

    def raw(i, h):
        await_bytes(pj.at[i, h, pl.ds(0, GROUP - 1)], s3r.at[i, h])
        for p in range(GROUP):
            r, c = 16 * (p % 4), half_ranks * (p // 4)
            pb[i, h, r:r + 16, c:c + half_ranks] = pj[i, h, p]
        proj = pb[i, h]
        for k, (j, who) in enumerate(((2 * yo, yp), (2 * yo + 1, ym), (2 * yp + 1, yp), (2 * ym, ym))):
            rs_s[i, h, k] = nt(proj, rows(u_v, j)).astype(BF16)
            send(rs_s.at[i, h, k], rs_r.at[i, h, k], rss.at[i, h, k], rsr.at[i, h, k], (state, who))
        part = nt(csm[...], proj)
        ms[i, h, 0:1, 0:hb] = part[0:1] + part[1:2] + part[2:3]
        for d, who in enumerate((yp, yo, ym)):
            send(ms.at[i, h], mr.at[i, h, d], mss.at[i, h], msr.at[i, h], (state, who))
        for k, j in enumerate((2 * yp, 2 * ym + 1, 2 * y, 2 * y + 1)):
            keep[h, k] = nt(proj, rows(u_v, j))

    def relay(i, h):
        for k, who in ((0, yp), (1, ym)):
            await_bytes(rs_r.at[i, h, k], rsr.at[i, h, k])
            rs_s[i, h, 4 + k] = (keep[h, k] + rs_r[i, h, k].astype(F32)).astype(BF16)
            send(rs_s.at[i, h, 4 + k], rs_r.at[i, h, 4 + k], rss.at[i, h, 4 + k], rsr.at[i, h, 4 + k], (state, who))

    def gather(i, h, k, j, who):
        send(w.at[i + 1, h, j], w.at[i + 1, h, j], ags.at[i, h, k], agr.at[i, h, k], (state, who))

    def own(i, h):
        await_bytes(mr.at[i, h], msr.at[i, h])
        mass = ms[i, h] + mr[i, h, 0] + mr[i, h, 1] + mr[i, h, 2]
        mass = mass.T[0:hb, 0:1] / states_all
        for part, (a, b, who) in enumerate(((3, 4, yp), (2, 5, ym))):
            for k in (a, b):
                await_bytes(rs_r.at[i, h, k], rsr.at[i, h, k])
            total = keep[h, 2 + part] + rs_r[i, h, a].astype(F32) + rs_r[i, h, b].astype(F32)
            new = (total / mass).astype(BF16).astype(F32)
            w[i + 1, h, 2 * y + part] = (emit[i, h, part] * new).astype(BF16)
            gather(i, h, part, 2 * y + part, who)
        gather(i, h, 2, 2 * y + 1, yp)
        gather(i, h, 3, 2 * y, ym)

    def landed(i, h, k):
        j = (2 * ym, 2 * yp + 1, 2 * ym + 1, 2 * yp, 2 * yo, 2 * yo + 1)[k]
        await_bytes(w.at[i + 1, h, j], agr.at[i, h, k])
        return j

    def forward(i, h):
        gather(i, h, 4, landed(i, h, 0), yp)
        gather(i, h, 5, landed(i, h, 1), ym)

    def project(i, h):
        def term(j):
            return nn(w[i, h, j], rows(v_v, j))

        total = term(2 * y) + term(2 * y + 1) + term(2 * ym) + term(2 * yp + 1)
        for k in range(2, 6):
            total += term(landed(i - 1, h, k))
        acc[h] = total

    def turn(i):
        t = STEPS - 1 - i

        def one(j, carry):
            both = jnp.concatenate([w[i, h, j] for h in range(HALVES)], axis=0)
            wn[pl.ds(pl.multiple_of(j * blk, blk), blk), pl.ds(pl.multiple_of(t * batch, batch), batch)] = both.T
            return carry

        lax.fori_loop(0, BLOCKS, one, 0)

    for h in range(HALVES):
        sum1(0, h)
    u_l.wait()
    columns1()
    sum2(0, 0)
    sum2(0, 1)
    columns2()

    ms[...] = jnp.zeros_like(ms)
    for t in range(STEPS - 1):
        find_words(t, id_cols[:, t:t + 1])
    for i in range(STEPS - 1):
        for part in range(2):
            logits = nt(words[STEPS - 2 - i], rows(semb_v, 2 * y + part))
            em = jnp.exp(logits - ln_v[2 * y + part])
            for h in range(HALVES):
                emit[i, h, part] = em[h * hb:(h + 1) * hb]
    emit[STEPS - 1] = jnp.ones_like(emit[STEPS - 1])
    sum3(0, 0)
    sum3(0, 1)
    columns3()
    fm_l.wait()

    a, b = 0, 1

    def body(i, carry):
        more = i < STEPS - 1
        raw(i, a)

        @pl.when(i > 0)
        def _():
            project(i, b)
            sum1(i, b)

        relay(i, a)

        @pl.when(i > 0)
        def _():
            sum2(i, b)

        fwd1(i)
        own(i, a)

        @pl.when(i > 0)
        def _():
            sum3(i, b)

        forward(i, a)
        raw(i, b)
        fwd2(i)

        @pl.when(more)
        def _():
            project(i + 1, a)
            sum1(i + 1, a)

        relay(i, b)

        @pl.when(more)
        def _():
            sum2(i + 1, a)

        turn(i)
        fwd3(i)
        own(i, b)

        @pl.when(more)
        def _():
            sum3(i + 1, a)

        forward(i, b)
        return carry

    lax.fori_loop(0, STEPS, body, 0)

    stores = [pltpu.make_async_copy(wn, wn_o, store.at[0])]
    stores[0].start()
    for i in range(STEPS):
        await_bytes(fj.at[i, pl.ds(0, GROUP - 1)], f3r.at[i])
        stores.append(pltpu.make_async_copy(fj.at[i], fw_o.at[STEPS - 1 - i], store.at[1 + i]))
        stores.append(pltpu.make_async_copy(pb.at[i], pb_o.at[STEPS - 1 - i], store.at[1 + STEPS + i]))
    for copy in stores[1:]:
        copy.start()
    for h in range(HALVES):
        for k in range(2, 6):
            landed(STEPS - 1, h, k)
    stores.append(pltpu.make_async_copy(w.at[STEPS], bt_o, store.at[1 + 2 * STEPS]))
    stores[-1].start()

    for k in range(2):
        await_bytes((cr1, cr2)[k], cs_s.at[k])

    def left_all(i, carry):
        await_bytes(fr1.at[i], f1s.at[i])
        await_bytes(fr2.at[i, pl.ds(0, zs - 1)], f2s.at[i])
        await_bytes(fj.at[i, pl.ds(0, GROUP - 1)], f3s.at[i])
        for h in range(HALVES):
            await_bytes(rb1.at[i, h], s1s.at[i, h])
            await_bytes(rb2.at[i, h, pl.ds(0, zs - 1)], s2s.at[i, h])
            await_bytes(pj.at[i, h, pl.ds(0, GROUP - 1)], s3s.at[i, h])
            await_bytes(mr.at[i, h], mss.at[i, h])
            for k in range(6):
                await_bytes(rs_s.at[i, h, k], rss.at[i, h, k])
                await_bytes(w.at[i + 1, h, k], ags.at[i, h, k])
        return carry

    lax.fori_loop(0, STEPS, left_all, 0)
    for copy in stores:
        copy.wait()


def gradients(count, fm, wn, pb, fw, bt, beta_o, left_o, right_o):
    hb = bt.shape[2]
    batch = HALVES * hb
    both = jnp.concatenate([bt[h, 0] for h in range(HALVES)], axis=0)
    beta_o[...] = both.T
    left_o[...] = (nn(fm[...], pb[...]) / count).astype(BF16)
    right_o[...] = (nn(wn[...], fw[...]) / count).astype(BF16)


def on_device(token_ids, word_emb, state_emb, log_norm, beta_last, forward_marg, trans_left, trans_right):
    states_n = lax.axis_size("state")
    zs = states_n // GROUP
    local, hidden = state_emb.shape
    states_all = states_n * local
    vocab = word_emb.shape[0]
    ranks = trans_left.shape[1]
    batch = beta_last.shape[1]
    hb = batch // HALVES
    blk = local // BLOCKS
    padded = -(-vocab // 1024) * 1024
    if padded == vocab:
        padded += 1024
    half_ranks = ranks // 2
    dma = pltpu.SemaphoreType.DMA
    vm = pltpu.VMEM
    scratch = [
        vm((STEPS, batch), jnp.int32), vm((padded, hidden), BF16), vm((local, hidden), BF16), vm((BLOCKS, 1, blk), F32),
        vm((local, batch), BF16), vm((local, STEPS * batch), BF16), vm((local, ranks), BF16), vm((local, ranks), BF16),
        vm((STEPS, batch, hidden), BF16), vm((STEPS + 1, HALVES, BLOCKS, hb, blk), BF16),
        vm((local, STEPS * batch), BF16), vm((STEPS, HALVES, 2, hb, blk), F32), vm((HALVES, hb, ranks), F32),
        vm((HALVES, 4, hb, blk), F32), vm((16, ranks), BF16), vm((STEPS, HALVES, hb, ranks), BF16),
        vm((STEPS, HALVES, GROUP, 16, half_ranks), BF16), vm((STEPS, HALVES, GROUP - 1, 16, half_ranks), BF16),
        vm((STEPS, HALVES, zs, 16, half_ranks), BF16), vm((STEPS, HALVES, GROUP, 16, half_ranks), BF16),
        vm((STEPS, GROUP, 16, ranks), BF16), vm((STEPS, GROUP - 1, 16, ranks), BF16),
        vm((STEPS, zs, 16, ranks), BF16), vm((STEPS, GROUP, 16, ranks), BF16),
        vm((2, 8, 128), F32), vm((GROUP - 1, 8, 128), F32), vm((zs - 1, 8, 128), F32),
        vm((STEPS, HALVES, 6, hb, blk), BF16), vm((STEPS, HALVES, 6, hb, blk), BF16),
        vm((STEPS, HALVES, 8, 128), F32), vm((STEPS, HALVES, RANKS - 1, 8, 128), F32),
        dma((8,)), dma((2 + 2 * STEPS,)),
        *[dma((STEPS, HALVES)) for _ in range(6)], *[dma((STEPS,)) for _ in range(6)], dma((2,)), dma((2,)),
        *[dma((STEPS, HALVES, 6)) for _ in range(4)], *[dma((STEPS, HALVES)) for _ in range(2)],
    ]
    anywhere = pl.BlockSpec(memory_space=pl.ANY)
    wn, pb, fw, bt = pl.pallas_call(
        functools.partial(recursion, states_all, zs),
        out_shape=(
            jax.ShapeDtypeStruct((local, STEPS * batch), BF16),
            jax.ShapeDtypeStruct((STEPS, HALVES, hb, ranks), BF16),
            jax.ShapeDtypeStruct((STEPS, GROUP, 16, ranks), BF16),
            jax.ShapeDtypeStruct((HALVES, BLOCKS, hb, blk), BF16),
        ),
        in_specs=[anywhere] * 8,
        out_specs=[anywhere] * 4,
        scratch_shapes=scratch,
        compiler_params=pltpu.CompilerParams(
            collective_id=0, has_side_effects=True, vmem_limit_bytes=56 * 2**20
        ),
        name="recursion",
    )(token_ids, word_emb, state_emb, log_norm.reshape(BLOCKS, 1, blk), beta_last, forward_marg, trans_left, trans_right)
    count = STEPS * batch
    whole = lambda shape: pl.BlockSpec(shape, lambda j: (0,) * len(shape))
    return pl.pallas_call(
        functools.partial(gradients, count),
        grid=(BLOCKS,),
        out_shape=(
            jax.ShapeDtypeStruct((local, batch), BF16),
            jax.ShapeDtypeStruct((local, ranks), BF16),
            jax.ShapeDtypeStruct((local, ranks), BF16),
        ),
        in_specs=[
            pl.BlockSpec((blk, count), lambda j: (j, 0)),
            pl.BlockSpec((blk, count), lambda j: (j, 0)),
            whole((count, ranks)),
            whole((count, ranks)),
            pl.BlockSpec((HALVES, 1, hb, blk), lambda j: (0, j, 0, 0)),
        ],
        out_specs=[
            pl.BlockSpec((blk, batch), lambda j: (j, 0)),
            pl.BlockSpec((blk, ranks), lambda j: (j, 0)),
            pl.BlockSpec((blk, ranks), lambda j: (j, 0)),
        ],
        compiler_params=pltpu.CompilerParams(vmem_limit_bytes=32 * 2**20),
        name="gradients",
    )(forward_marg, wn, pb.reshape(count, ranks), fw.reshape(count, ranks), bt)


def solution(mesh):
    placed = (
        P(), P(), P("state", None), P("state"), P("state", None), P("state", None), P("state", "rank"), P("state", "rank"),
    )
    return jax.shard_map(
        on_device,
        mesh=mesh,
        in_specs=placed,
        out_specs=(P("state", None), P("state", "rank"), P("state", "rank")),
        check_vma=False,
    )
```

time: 666 us -> 128 us (0.19)
  blocking collectives: 578 us -> 0 us
  Pallas kernels: 0 us -> 120 us
  matrix products: 44.3 us -> 0 us
  local copies, waits for them, and re-layouts: 22 us -> 5.1 us
  between operations: 13.9 us -> 0.67 us
    psum x6 -> x0, blocking collectives: 578 us -> none  [the longest x3 373 us: on_device(): projb = lax.psum(proj_part, 'state').astype(jnp.bfloat16)]
    pallas_call x0 -> x2, Pallas kernels: none -> 120 us  [the longest x1 113 us: on_device(): pl.pallas_call(functools.partial(recursion, states_all, zs), out_shape=(j...]
    dot_general x15 -> x0, matrix products: 44.3 us -> none  [the longest x3 14.9 us: on_device(): lax.dot_general(trans_left, projb, (((1,), (1,)), ((), ())), preferred_el...]
    unnamed x17 -> x10, local copies, waits for them, and re-layouts: 13.9 us -> 5.1 us
    gather x3 -> x0, local copies, waits for them, and re-layouts: 8.1 us -> none  [on_device(): words = jnp.take(word_emb, token_ids[step], axis=0)]
  transfers between devices with their start and end apart: 4 -> 0, of which waited for: 0 -> 0; matrix products, arithmetic and copies ran while one was open for 6% -> 0% of each run, Pallas kernels for 0% -> 0%
where the time goes in v1:
time: 128 us; the launch traced here: 126 us
  Pallas kernels  120 us (94%)
  local copies, waits for them, and re-layouts  5.1 us (4%)
    pallas_call x1, Pallas kernels, on_device(): pl.pallas_call(functools.partial(recursion, states_all, zs), out_shape=(j...  113 us
    pallas_call x1, Pallas kernels, on_device(): pl.pallas_call(functools.partial(gradients, count), grid=(BLOCKS,), out_s...  7.09 us
    unnamed x10, local copies, waits for them, and re-layouts  5.1 us

profile of v1, /device:TPU:1, one launch (start us, length us, event | category | flops | bytes accessed | tf_op | source)
XLA Modules:
  0.0 126.2 jit_solution(16952238323991583230)
XLA Ops:
  0.6 0.0 copy-start
  0.6 113.3 %recursion.1 = (bf16[4096,384]{1,0:T(8,128)(2,1)}, bf16[3,2,64,512]{3,2,1,0:T(8,128)(2,1)}, bf16[3,8,16,512]{3,2,1,0:T(8,128)(2,1)}, bf16[2,8,64,512]{3,2,1,0:T(8,128)(2,1)}) custom-call(s32[3,128]{1,0:T(4,128)} %ids.1, bf16[10000,128]{1,0:T(8,128)(2,1)} %word_emb.1, bf16[4096,128]{1,0:T(8,128)(2,1)} %semb.1, f32[8,1,512]{2,1,0:T(1,128)} %bitcast.5, ...), custom_call_target="tpu_custom_call" | custom-call | tf_op jit(solution)/shard_map/recursion/pallas_call | solution.py:440
  114.0 0.0 copy-done
  114.0 0.0 copy-start.1
  114.0 1.9 %copy-done.1 = bf16[4096,384]{1,0:T(8,128)(2,1)S(1)} copy-done((bf16[4096,384]{1,0:T(8,128)(2,1)S(1)}, bf16[4096,384]{1,0:T(8,128)(2,1)}, u32[]{:S(2)}) %copy-start.1) | copy-done | bytes 3145752
  115.9 0.0 copy-start.2
  115.9 1.2 copy-done.2
  117.1 0.0 copy-start.3
  117.1 1.0 copy-done.3
  118.1 0.0 copy-start.4
  118.1 1.0 copy-done.4
  119.1 7.1 %gradients.1 = (bf16[4096,128]{1,0:T(8,128)(2,1)}, bf16[4096,512]{1,0:T(8,128)(2,1)}, bf16[4096,512]{1,0:T(8,128)(2,1)}) custom-call(bf16[4096,384]{1,0:T(8,128)(2,1)S(1)} %copy-done, bf16[4096,384]{1,0:T(8,128)(2,1)S(1)} %copy-done.1, bf16[384,512]{1,0:T(8,128)(2,1)S(1)} %bitcast.3, bf16[384,512]{1,0:T(8,128)(2,1)S(1)} %bitcast.4, ...), custom_call_target="tpu_custom_call" | custom-call | tf_op jit(solution)/shard_map/gradients/pallas_call | solution.py:458
Async XLA Ops:
  0.6 113.3 %copy-start = (bf16[4096,384]{1,0:T(8,128)(2,1)S(1)}, bf16[4096,384]{1,0:T(8,128)(2,1)}, u32[]{:S(2)}) copy-start(bf16[4096,384]{1,0:T(8,128)(2,1)} %fm.3) | copy-start | bytes 9437188
  114.0 1.9 %copy-start.1 = (bf16[4096,384]{1,0:T(8,128)(2,1)S(1)}, bf16[4096,384]{1,0:T(8,128)(2,1)}, u32[]{:S(2)}) copy-start(bf16[4096,384]{1,0:T(8,128)(2,1)} %get-tuple-element.7.wn) | copy-start | bytes 9437188
  115.9 1.2 copy-start.2
  117.1 1.0 copy-start.3
  118.1 1.0 copy-start.4

commit v2 on v1

v2 whole, which is shorter than its diff:
```python
import functools

import jax
import jax.numpy as jnp
from jax import lax
from jax.experimental import pallas as pl
from jax.experimental.pallas import tpu as pltpu
from jax.sharding import PartitionSpec as P

MESH = pl.DeviceIdType.MESH
F32 = jnp.float32
BF16 = jnp.bfloat16
GROUP = 8
RANKS = 4
BLOCKS = 2 * RANKS
HALVES = 2
STEPS = 3


def nn(a, b):
    return lax.dot_general(a, b, (((1,), (0,)), ((), ())), preferred_element_type=F32)


def nt(a, b):
    return lax.dot_general(a, b, (((1,), (1,)), ((), ())), preferred_element_type=F32)


def recursion(
    states_all, zs,
    ids, word_emb, semb, ln, beta, fm, left, right,
    left_o, right_o, bt_o,
    ids_s, ids_v, emb_v, semb_v, ln_v, beta_v, fm_v, u_v, v_v,
    tiles_v, words, w, wn, emit, acc, keep, csm, pb,
    cb, cr, xb, fs1, fr1, fr2, fj, cs, cr1, cr2,
    rs_s, rs_r, ms, mr,
    load, c1s, c1r, xs, xr, c2s, c2r, f1s, f1r, f2s, f2r, f3s, f3r, cs_s, cs_r,
    rss, rsr, ags, agr, mss, msr,
):
    state = lax.axis_index("state")
    y = lax.axis_index("rank")
    chips = zs * GROUP // 2
    g = lax.rem(state, GROUP)
    z = state // GROUP
    chip = state // 2
    core = lax.rem(state, 2)
    yp, yo, ym = lax.rem(y + 1, RANKS), lax.rem(y + 2, RANKS), lax.rem(y + 3, RANKS)
    local, ranks = left.shape
    blk = local // BLOCKS
    hb = w.shape[3]
    half = hb // 2
    batch = HALVES * hb
    hidden = semb.shape[1]
    count = STEPS * batch

    loads = [
        (ids, ids_s), (ids, ids_v), (word_emb, emb_v), (left, u_v), (semb, semb_v), (ln, ln_v), (beta, beta_v),
        (right, v_v), (fm, fm_v),
    ]
    loads = [pltpu.make_async_copy(src, dst, load.at[k]) for k, (src, dst) in enumerate(loads)]
    ids_l, idv_l, emb_l, u_l, semb_l, ln_l, beta_l, v_l, fm_l = loads
    for copy in loads[:8]:
        copy.start()

    def group_peer(d):
        p = lax.rem(g + d, GROUP)
        return p, (z * GROUP + p, y)

    def z_peer(d):
        return (lax.rem(z + d, zs) * GROUP + g, y)

    def chip_peer(d):
        return (2 * lax.rem(chip + d, chips) + core, y)

    partner = (2 * chip + 1 - core, y)
    barrier = pltpu.get_barrier_semaphore()
    greeted = [group_peer(d)[1] for d in range(1, GROUP)] + [(state, other) for other in (yp, yo, ym)]
    for dz in range(1, zs):
        for dx in range(0, GROUP, 2):
            greeted.append((lax.rem(z + dz, zs) * GROUP + lax.rem(g + dx, GROUP), y))
    for who in greeted:
        pl.semaphore_signal(barrier, inc=1, device_id=who, device_id_type=MESH)

    def send(src, dst, send_sem, recv_sem, who):
        pltpu.make_async_remote_copy(
            src_ref=src, dst_ref=dst, send_sem=send_sem, recv_sem=recv_sem, device_id=who, device_id_type=MESH
        ).start()

    def await_bytes(ref, sem):
        pltpu.make_async_copy(ref, ref, sem).wait()

    def rows(ref, j):
        return ref[pl.ds(pl.multiple_of(j * blk, blk), blk), :]

    lines = ranks // 128

    def columns1():
        def one(j, total):
            return total + nn(jnp.ones((16, blk), BF16), rows(u_v, j))

        total = lax.fori_loop(0, BLOCKS, one, jnp.zeros((16, ranks), F32))
        cs[...] = jnp.zeros_like(cs)
        for c in range(lines):
            cs[0, c:c + 1, :] = total[0:1, 128 * c:128 * c + 128]
        pl.semaphore_wait(barrier, len(greeted))
        for d in range(1, GROUP):
            send(cs.at[0], cr1.at[d - 1], cs_s.at[0], cs_r.at[0], group_peer(d)[1])

    def columns2():
        await_bytes(cr1, cs_r.at[0])
        total = cs[0]
        for d in range(GROUP - 1):
            total += cr1[d]
        cs[1] = total
        for d in range(1, zs):
            send(cs.at[1], cr2.at[d - 1], cs_s.at[1], cs_r.at[1], z_peer(d))

    def columns3():
        await_bytes(cr2, cs_r.at[1])
        total = cs[1]
        for d in range(zs - 1):
            total += cr2[d]
        line = jnp.concatenate([total[c:c + 1] for c in range(lines)], axis=1)
        high = line.astype(BF16)
        rest = line - high.astype(F32)
        mid = rest.astype(BF16)
        low = (rest - mid.astype(F32)).astype(BF16)
        parts = [x.astype(F32) for x in (high, mid, low)] + [jnp.zeros((13, ranks), F32)]
        csm[...] = jnp.concatenate(parts, axis=0).astype(BF16)

    def find_words(t):
        def one(k, carry):
            tiles_v[k] = emb_v[lax.shift_right_logical(ids_s[t, k], 4)]
            return carry

        lax.fori_loop(0, batch, one, 0, unroll=8)
        lane = lax.broadcasted_iota(jnp.int32, (batch, 16 * batch), 1).astype(F32)
        pick = jnp.where(lane == place[:, t:t + 1], 1.0, 0.0).astype(BF16)
        words[t] = nn(pick, tiles_v[...].reshape(16 * batch, hidden)).astype(BF16)

    ids_l.wait()
    idv_l.wait()
    inside = jnp.bitwise_and(ids_v[...], 15) + 16 * lax.broadcasted_iota(jnp.int32, (STEPS, batch), 1)
    place = jnp.concatenate([inside.astype(F32), jnp.zeros((8 - STEPS, batch), F32)], axis=0).T
    emb_l.wait()
    find_words(STEPS - 1)
    u_l.wait()
    columns1()

    semb_l.wait()
    ln_l.wait()
    beta_l.wait()
    v_l.wait()
    fm_l.start()
    eye = jnp.where(
        lax.broadcasted_iota(jnp.int32, (batch, batch), 0) == lax.broadcasted_iota(jnp.int32, (batch, batch), 1), 1.0, 0.0
    ).astype(BF16)

    def first(j, total):
        logits = nt(words[STEPS - 1], rows(semb_v, j))
        em = jnp.exp(logits - ln_v[j])
        wt = (em * nt(eye, rows(beta_v, j))).astype(BF16)
        for h in range(HALVES):
            w[0, h, j] = wt[h * hb:(h + 1) * hb]
        return total + nn(wt, rows(v_v, j))

    total = lax.fori_loop(0, BLOCKS, first, jnp.zeros((batch, ranks), F32))
    for h in range(HALVES):
        acc[h] = total[h * hb:(h + 1) * hb]

    def sum1(i, h):
        cb[i, h] = acc[h, pl.ds(pl.multiple_of(half * (1 - core), half), half), :].astype(BF16)
        send(cb.at[i, h], cr.at[i, h], c1s.at[i, h], c1r.at[i, h], partner)

    def sum2(i, h):
        await_bytes(cr.at[i, h], c1r.at[i, h])
        mine = acc[h, pl.ds(pl.multiple_of(half * core, half), half), :]
        xb[i, h, chip] = (mine + cr[i, h].astype(F32)).astype(BF16)
        for d in range(1, chips):
            send(xb.at[i, h, chip], xb.at[i, h, chip], xs.at[i, h], xr.at[i, h], chip_peer(d))

    def sum3(i, h):
        await_bytes(xb.at[i, h, pl.ds(0, chips - 1)], xr.at[i, h])
        total = xb[i, h, 0].astype(F32)
        for d in range(1, chips):
            total += xb[i, h, d].astype(F32)
        pb[STEPS - 1 - i, h, core] = total.astype(BF16)
        place_of = pb.at[STEPS - 1 - i, h, core]
        send(place_of, place_of, c2s.at[i, h], c2r.at[i, h], partner)

    def fwd1(i):
        t = STEPS - 1 - i

        def one(j, total):
            cols = fm_v[pl.ds(pl.multiple_of(j * blk, blk), blk), pl.ds(pl.multiple_of(t * batch, batch), batch)]
            return total + nn(cols.T, rows(u_v, j))

        total = lax.fori_loop(0, BLOCKS, one, jnp.zeros((batch, ranks), F32))
        for p in range(GROUP):
            fs1[i, p] = total[16 * p:16 * p + 16].astype(BF16)
        for d in range(1, GROUP):
            p, who = group_peer(d)
            send(fs1.at[i, p], fr1.at[i, d - 1], f1s.at[i], f1r.at[i], who)

    def fwd2(i):
        await_bytes(fr1.at[i], f1r.at[i])
        total = fs1[i, g].astype(F32)
        for d in range(GROUP - 1):
            total += fr1[i, d].astype(F32)
        fr2[i, z] = total.astype(BF16)
        for d in range(1, zs):
            send(fr2.at[i, z], fr2.at[i, z], f2s.at[i], f2r.at[i], z_peer(d))

    def fwd3(i):
        t = STEPS - 1 - i
        await_bytes(fr2.at[i, pl.ds(0, zs - 1)], f2r.at[i])
        total = fr2[i, 0].astype(F32)
        for d in range(1, zs):
            total += fr2[i, d].astype(F32)
        fj[t, g] = (total / states_all).astype(BF16)
        for d in range(1, GROUP):
            send(fj.at[t, g], fj.at[t, g], f3s.at[i], f3r.at[i], group_peer(d)[1])

    def raw(i, h):
        await_bytes(pb.at[STEPS - 1 - i, h, 0], c2r.at[i, h])
        proj = pb[STEPS - 1 - i, h].reshape(hb, ranks)
        sums = nt(csm[...], proj)
        ms[i, h, 0:1, 0:hb] = sums[0:1] + sums[1:2] + sums[2:3]
        for d, who in enumerate((yp, yo, ym)):
            send(ms.at[i, h], mr.at[i, h, d], mss.at[i, h], msr.at[i, h], (state, who))
        for part in range(2):
            for d, who in ((1, yo), (0, yp), (2, ym)):
                rs_s[i, h, part, d] = nt(proj, rows(u_v, 2 * who + part)).astype(BF16)
                send(rs_s.at[i, h, part, d], rs_r.at[i, h, part, d], rss.at[i, h, part], rsr.at[i, h, part], (state, who))
        for part in range(2):
            keep[h, part] = nt(proj, rows(u_v, 2 * y + part))

    def mass_of(i, h):
        await_bytes(mr.at[i, h], msr.at[i, h])
        mass = ms[i, h] + mr[i, h, 0] + mr[i, h, 1] + mr[i, h, 2]
        return mass.T[0:hb, 0:1] / states_all

    def own(i, h):
        mass = mass_of(i, h)
        for part in range(2):
            await_bytes(rs_r.at[i, h, part], rsr.at[i, h, part])
            total = keep[h, part]
            for d in range(RANKS - 1):
                total += rs_r[i, h, part, d].astype(F32)
            new = (total / mass).astype(BF16).astype(F32)
            j = 2 * y + part
            w[i + 1, h, j] = (emit[i, h, part] * new).astype(BF16)
            for who in (yo, yp, ym):
                send(w.at[i + 1, h, j], w.at[i + 1, h, j], ags.at[i, h, part], agr.at[i, h, part], (state, who))

    def landed(i, h, part):
        await_bytes(w.at[i + 1, h, pl.ds(0, RANKS - 1)], agr.at[i, h, part])

    def project(i, h):
        def term(j):
            return nn(w[i, h, j], rows(v_v, j))

        total = term(2 * y) + term(2 * y + 1)
        for part in range(2):
            landed(i - 1, h, part)
            for who in (yp, yo, ym):
                total += term(2 * who + part)
        acc[h] = total
        sum1(i, h)

    def turn(i):
        t = STEPS - 1 - i

        def one(j, carry):
            both = jnp.concatenate([w[i, h, j] for h in range(HALVES)], axis=0)
            wn[pl.ds(pl.multiple_of(j * blk, blk), blk), pl.ds(pl.multiple_of(t * batch, batch), batch)] = both.T
            return carry

        lax.fori_loop(0, BLOCKS, one, 0)

    def gradients():
        for i in range(STEPS):
            await_bytes(fj.at[i, pl.ds(0, GROUP - 1)], f3r.at[i])
        proj = pb[...].reshape(count, ranks)
        fwd = fj[...].reshape(count, ranks)

        def one(j, carry):
            at = pl.ds(pl.multiple_of(j * blk, blk), blk)
            left_o[at, :] = (nn(fm_v[at, :], proj) / count).astype(BF16)
            right_o[at, :] = (nn(wn[at, :], fwd) / count).astype(BF16)
            return carry

        lax.fori_loop(0, BLOCKS, one, 0)

    a, b = 0, 1
    sum1(0, a)
    sum1(0, b)
    columns2()
    sum2(0, a)

    ms[...] = jnp.zeros_like(ms)
    for t in range(STEPS - 1):
        find_words(t)
    for i in range(STEPS - 1):
        for part in range(2):
            logits = nt(words[STEPS - 2 - i], rows(semb_v, 2 * y + part))
            em = jnp.exp(logits - ln_v[2 * y + part])
            for h in range(HALVES):
                emit[i, h, part] = em[h * hb:(h + 1) * hb]
    emit[STEPS - 1] = jnp.ones_like(emit[STEPS - 1])
    columns3()
    fm_l.wait()
    fwd1(0)
    sum2(0, b)
    sum3(0, a)

    def body(i, carry):
        more = i < STEPS - 1
        raw(i, a)

        @pl.when(i > 0)
        def _():
            sum2(i, b)

        fwd2(i)
        turn(i)

        @pl.when(more)
        def _():
            fwd1(i + 1)

        own(i, a)
        sum3(i, b)
        raw(i, b)
        fwd3(i)

        @pl.when(more)
        def _():
            project(i + 1, a)
            sum2(i + 1, a)

        @pl.when(i == STEPS - 1)
        def _():
            gradients()

        own(i, b)

        @pl.when(more)
        def _():
            project(i + 1, b)
            sum3(i + 1, a)

        return carry

    lax.fori_loop(0, STEPS, body, 0)

    for h in range(HALVES):
        for part in range(2):
            landed(STEPS - 1, h, part)
    bt_o[...] = w[STEPS]

    for k in range(2):
        await_bytes((cr1, cr2)[k], cs_s.at[k])

    def left_all(i, carry):
        await_bytes(fr1.at[i], f1s.at[i])
        await_bytes(fr2.at[i, pl.ds(0, zs - 1)], f2s.at[i])
        await_bytes(fj.at[i, pl.ds(0, GROUP - 1)], f3s.at[i])
        for h in range(HALVES):
            await_bytes(cr.at[i, h], c1s.at[i, h])
            await_bytes(xb.at[i, h, pl.ds(0, chips - 1)], xs.at[i, h])
            await_bytes(pb.at[i, h, 0], c2s.at[i, h])
            await_bytes(mr.at[i, h], mss.at[i, h])
            for part in range(2):
                await_bytes(rs_r.at[i, h, part], rss.at[i, h, part])
                await_bytes(w.at[i + 1, h, pl.ds(0, RANKS - 1)], ags.at[i, h, part])
        return carry

    lax.fori_loop(0, STEPS, left_all, 0)


def finish(bt, left, right, beta_o, left_o, right_o, beta_v, sems):
    copies = [pltpu.make_async_copy(left, left_o, sems.at[0]), pltpu.make_async_copy(right, right_o, sems.at[1])]
    for copy in copies:
        copy.start()
    blk = bt.shape[3]

    def one(j, carry):
        both = jnp.concatenate([bt[h, j] for h in range(HALVES)], axis=0)
        beta_v[pl.ds(pl.multiple_of(j * blk, blk), blk), :] = both.T
        return carry

    lax.fori_loop(0, BLOCKS, one, 0)
    copies.append(pltpu.make_async_copy(beta_v, beta_o, sems.at[2]))
    copies[2].start()
    for copy in copies:
        copy.wait()


def on_device(token_ids, word_emb, state_emb, log_norm, beta_last, forward_marg, trans_left, trans_right):
    states_n = lax.axis_size("state")
    zs = states_n // GROUP
    chips = states_n // 2
    local, hidden = state_emb.shape
    states_all = states_n * local
    vocab = word_emb.shape[0]
    ranks = trans_left.shape[1]
    batch = beta_last.shape[1]
    hb = batch // HALVES
    blk = local // BLOCKS
    dma = pltpu.SemaphoreType.DMA
    vm = pltpu.VMEM
    scratch = [
        pltpu.SMEM((STEPS, batch), jnp.int32), vm((STEPS, batch), jnp.int32), vm((vocab // 16, 16, hidden), BF16),
        vm((local, hidden), BF16), vm((BLOCKS, 1, blk), F32), vm((local, batch), BF16), vm((local, STEPS * batch), BF16),
        vm((local, ranks), BF16), vm((local, ranks), BF16),
        vm((batch, 16, hidden), BF16), vm((STEPS, batch, hidden), BF16), vm((STEPS + 1, HALVES, BLOCKS, hb, blk), BF16),
        vm((local, STEPS * batch), BF16), vm((STEPS, HALVES, 2, hb, blk), F32), vm((HALVES, hb, ranks), F32),
        vm((HALVES, 2, hb, blk), F32), vm((16, ranks), BF16), vm((STEPS, HALVES, 2, hb // 2, ranks), BF16),
        vm((STEPS, HALVES, hb // 2, ranks), BF16), vm((STEPS, HALVES, hb // 2, ranks), BF16),
        vm((STEPS, HALVES, chips, hb // 2, ranks), BF16),
        vm((STEPS, GROUP, 16, ranks), BF16), vm((STEPS, GROUP - 1, 16, ranks), BF16),
        vm((STEPS, zs, 16, ranks), BF16), vm((STEPS, GROUP, 16, ranks), BF16),
        vm((2, 8, 128), F32), vm((GROUP - 1, 8, 128), F32), vm((zs - 1, 8, 128), F32),
        vm((STEPS, HALVES, 2, RANKS - 1, hb, blk), BF16), vm((STEPS, HALVES, 2, RANKS - 1, hb, blk), BF16),
        vm((STEPS, HALVES, 8, 128), F32), vm((STEPS, HALVES, RANKS - 1, 8, 128), F32),
        dma((9,)),
        *[dma((STEPS, HALVES)) for _ in range(6)], *[dma((STEPS,)) for _ in range(6)], dma((2,)), dma((2,)),
        *[dma((STEPS, HALVES, 2)) for _ in range(4)], *[dma((STEPS, HALVES)) for _ in range(2)],
    ]
    anywhere = pl.BlockSpec(memory_space=pl.ANY)
    inside = pl.BlockSpec(memory_space=pltpu.VMEM)
    left, right, bt = pl.pallas_call(
        functools.partial(recursion, states_all, zs),
        out_shape=(vm((local, ranks), BF16), vm((local, ranks), BF16), vm((HALVES, BLOCKS, hb, blk), BF16)),
        in_specs=[anywhere] * 8,
        out_specs=[inside] * 3,
        scratch_shapes=scratch,
        compiler_params=pltpu.CompilerParams(
            collective_id=0, has_side_effects=True, vmem_limit_bytes=46 * 2**20
        ),
        name="recursion",
    )(
        token_ids, word_emb.reshape(vocab // 16, 16, hidden), state_emb, log_norm.reshape(BLOCKS, 1, blk), beta_last,
        forward_marg, trans_left, trans_right,
    )
    beta, left, right = pl.pallas_call(
        finish,
        out_shape=(
            jax.ShapeDtypeStruct((local, batch), BF16),
            jax.ShapeDtypeStruct((local, ranks), BF16),
            jax.ShapeDtypeStruct((local, ranks), BF16),
        ),
        in_specs=[inside] * 3,
        out_specs=[anywhere] * 3,
        scratch_shapes=[vm((local, batch), BF16), dma((3,))],
        compiler_params=pltpu.CompilerParams(vmem_limit_bytes=16 * 2**20),
        name="finish",
    )(bt, left, right)
    return beta, left, right


def solution(mesh):
    placed = (
        P(), P(), P("state", None), P("state"), P("state", None), P("state", None), P("state", "rank"), P("state", "rank"),
    )
    return jax.shard_map(
        on_device,
        mesh=mesh,
        in_specs=placed,
        out_specs=(P("state", None), P("state", "rank"), P("state", "rank")),
        check_vma=False,
    )
```

time: 128 us -> 120 us (0.938); the launches traced: 126 us -> 120 us
  local copies, waits for them, and re-layouts: 5.1 us -> 0 us
    unnamed x10 -> x0, local copies, waits for them, and re-layouts: 5.1 us -> none
where the time goes in v2:
time: 120 us
  Pallas kernels  119 us (99%)
    pallas_call x1, Pallas kernels, on_device(): pl.pallas_call(functools.partial(recursion, states_all, zs), out_shape=(v...  116 us
    pallas_call x1, Pallas kernels, on_device(): pl.pallas_call(finish, out_shape=(jax.ShapeDtypeStruct((local, batch), BF...  3.64 us

profile of v2, /device:TPU:1, one launch (start us, length us, event | category | flops | bytes accessed | tf_op | source)
XLA Modules:
  0.0 119.8 jit_solution(10953533317295295580)
XLA Ops:
  0.6 115.5 %recursion.1 = (bf16[4096,512]{1,0:T(8,128)(2,1)S(1)}, bf16[4096,512]{1,0:T(8,128)(2,1)S(1)}, bf16[2,8,64,512]{3,2,1,0:T(8,128)(2,1)S(1)}) custom-call(s32[3,128]{1,0:T(4,128)} %ids.1, bf16[625,16,128]{2,1,0:T(8,128)(2,1)} %bitcast.2, bf16[4096,128]{1,0:T(8,128)(2,1)} %semb.1, f32[8,1,512]{2,1,0:T(1,128)} %bitcast.3, bf16[4096,128]{1,0:T(8,128)(2,1)} %beta.1, ...), custom_call_target="tpu_custom_call" | custom-call | tf_op jit(solution)/shard_map/recursion/pallas_call | solution.py:432
  116.2 3.6 %finish.1 = (bf16[4096,128]{1,0:T(8,128)(2,1)}, bf16[4096,512]{1,0:T(8,128)(2,1)}, bf16[4096,512]{1,0:T(8,128)(2,1)}) custom-call(bf16[2,8,64,512]{3,2,1,0:T(8,128)(2,1)S(1)} %get-tuple-element.6.bt, bf16[4096,512]{1,0:T(8,128)(2,1)S(1)} %get-tuple-element.7.left, bf16[4096,512]{1,0:T(8,128)(2,1)S(1)} %get-tuple-element.8.right), custom_call_target="tpu_custom_call" | custom-call | tf_op jit(solution)/shard_map/finish/pallas_call | solution.py:446

commit v3 on v2

--- a/solution.py
+++ b/solution.py
@@ -13,7 +13,7 @@
 GROUP = 8
 RANKS = 4
 BLOCKS = 2 * RANKS
-HALVES = 2
+CHAINS = 4
 STEPS = 3
 
 
@@ -31,7 +31,7 @@
     left_o, right_o, bt_o,
     ids_s, ids_v, emb_v, semb_v, ln_v, beta_v, fm_v, u_v, v_v,
     tiles_v, words, w, wn, emit, acc, keep, csm, pb,
-    cb, cr, xb, fs1, fr1, fr2, fj, cs, cr1, cr2,
+    cb, cr, xb, facc, fs1, fr1, fr2, fj, cs, cr1, cr2,
     rs_s, rs_r, ms, mr,
     load, c1s, c1r, xs, xr, c2s, c2r, f1s, f1r, f2s, f2r, f3s, f3r, cs_s, cs_r,
     rss, rsr, ags, agr, mss, msr,
@@ -48,17 +48,21 @@
     blk = local // BLOCKS
     hb = w.shape[3]
     half = hb // 2
-    batch = HALVES * hb
+    batch = CHAINS * hb
     hidden = semb.shape[1]
     count = STEPS * batch
 
     loads = [
-        (ids, ids_s), (ids, ids_v), (word_emb, emb_v), (left, u_v), (semb, semb_v), (ln, ln_v), (beta, beta_v),
-        (right, v_v), (fm, fm_v),
+        (ids, ids_s), (ids, ids_v), (word_emb, emb_v), (semb, semb_v), (ln, ln_v), (beta, beta_v), (left, u_v), (fm, fm_v),
     ]
     loads = [pltpu.make_async_copy(src, dst, load.at[k]) for k, (src, dst) in enumerate(loads)]
-    ids_l, idv_l, emb_l, u_l, semb_l, ln_l, beta_l, v_l, fm_l = loads
-    for copy in loads[:8]:
+    ids_l, idv_l, emb_l, semb_l, ln_l, beta_l, u_l, fm_l = loads
+
+    def v_l(j):
+        at = pl.ds(pl.multiple_of(j * blk, blk), blk)
+        return pltpu.make_async_copy(right.at[at], v_v.at[at], load.at[8 + j])
+
+    for copy in loads[:6] + [v_l(j) for j in range(BLOCKS)] + loads[6:]:
         copy.start()
 
     def group_peer(d):
@@ -88,6 +92,13 @@
     def await_bytes(ref, sem):
         pltpu.make_async_copy(ref, ref, sem).wait()
 
+    def each(first, last, act):
+        def one(d, carry):
+            act(d)
+            return carry
+
+        lax.fori_loop(first, last, one, 0, unroll=True)
+
     def rows(ref, j):
         return ref[pl.ds(pl.multiple_of(j * blk, blk), blk), :]
 
@@ -101,7 +112,6 @@
         cs[...] = jnp.zeros_like(cs)
         for c in range(lines):
             cs[0, c:c + 1, :] = total[0:1, 128 * c:128 * c + 128]
-        pl.semaphore_wait(barrier, len(greeted))
         for d in range(1, GROUP):
             send(cs.at[0], cr1.at[d - 1], cs_s.at[0], cs_r.at[0], group_peer(d)[1])
 
@@ -143,14 +153,10 @@
     place = jnp.concatenate([inside.astype(F32), jnp.zeros((8 - STEPS, batch), F32)], axis=0).T
     emb_l.wait()
     find_words(STEPS - 1)
-    u_l.wait()
-    columns1()
 
     semb_l.wait()
     ln_l.wait()
     beta_l.wait()
-    v_l.wait()
-    fm_l.start()
     eye = jnp.where(
         lax.broadcasted_iota(jnp.int32, (batch, batch), 0) == lax.broadcasted_iota(jnp.int32, (batch, batch), 1), 1.0, 0.0
     ).astype(BF16)
@@ -159,13 +165,16 @@
         logits = nt(words[STEPS - 1], rows(semb_v, j))
         em = jnp.exp(logits - ln_v[j])
         wt = (em * nt(eye, rows(beta_v, j))).astype(BF16)
-        for h in range(HALVES):
+        for h in range(CHAINS):
             w[0, h, j] = wt[h * hb:(h + 1) * hb]
+        v_l(j).wait()
         return total + nn(wt, rows(v_v, j))
 
-    total = lax.fori_loop(0, BLOCKS, first, jnp.zeros((batch, ranks), F32))
-    for h in range(HALVES):
+    total = lax.fori_loop(0, BLOCKS, first, jnp.zeros((batch, ranks), F32), unroll=2)
+    for h in range(CHAINS):
         acc[h] = total[h * hb:(h + 1) * hb]
+
+    pl.semaphore_wait(barrier, len(greeted))
 
     def sum1(i, h):
         cb[i, h] = acc[h, pl.ds(pl.multiple_of(half * (1 - core), half), half), :].astype(BF16)
@@ -175,8 +184,8 @@
         await_bytes(cr.at[i, h], c1r.at[i, h])
         mine = acc[h, pl.ds(pl.multiple_of(half * core, half), half), :]
         xb[i, h, chip] = (mine + cr[i, h].astype(F32)).astype(BF16)
-        for d in range(1, chips):
-            send(xb.at[i, h, chip], xb.at[i, h, chip], xs.at[i, h], xr.at[i, h], chip_peer(d))
+        mine = xb.at[i, h, chip]
+        each(1, chips, lambda d: send(mine, mine, xs.at[i, h], xr.at[i, h], chip_peer(d)))
 
     def sum3(i, h):
         await_bytes(xb.at[i, h, pl.ds(0, chips - 1)], xr.at[i, h])
@@ -187,19 +196,33 @@
         place_of = pb.at[STEPS - 1 - i, h, core]
         send(place_of, place_of, c2s.at[i, h], c2r.at[i, h], partner)
 
-    def fwd1(i):
+    def fwd1(i, part):
         t = STEPS - 1 - i
 
         def one(j, total):
             cols = fm_v[pl.ds(pl.multiple_of(j * blk, blk), blk), pl.ds(pl.multiple_of(t * batch, batch), batch)]
             return total + nn(cols.T, rows(u_v, j))
 
-        total = lax.fori_loop(0, BLOCKS, one, jnp.zeros((batch, ranks), F32))
-        for p in range(GROUP):
-            fs1[i, p] = total[16 * p:16 * p + 16].astype(BF16)
-        for d in range(1, GROUP):
-            p, who = group_peer(d)
-            send(fs1.at[i, p], fr1.at[i, d - 1], f1s.at[i], f1r.at[i], who)
+        @pl.when(part == 0)
+        def _():
+            facc[...] = jnp.zeros_like(facc)
+
+        count = BLOCKS // CHAINS
+        total = facc[...]
+        for j in range(count):
+            total = one(part * count + j, total)
+        facc[...] = total
+
+        @pl.when(part == CHAINS - 1)
+        def _():
+            for p in range(GROUP):
+                fs1[i, p] = facc[16 * p:16 * p + 16].astype(BF16)
+
+            def out(d):
+                p, who = group_peer(d)
+                send(fs1.at[i, p], fr1.at[i, d - 1], f1s.at[i], f1r.at[i], who)
+
+            each(1, GROUP, out)
 
     def fwd2(i):
         await_bytes(fr1.at[i], f1r.at[i])
@@ -217,20 +240,27 @@
         for d in range(1, zs):
             total += fr2[i, d].astype(F32)
         fj[t, g] = (total / states_all).astype(BF16)
-        for d in range(1, GROUP):
-            send(fj.at[t, g], fj.at[t, g], f3s.at[i], f3r.at[i], group_peer(d)[1])
+        each(1, GROUP, lambda d: send(fj.at[t, g], fj.at[t, g], f3s.at[i], f3r.at[i], group_peer(d)[1]))
 
     def raw(i, h):
         await_bytes(pb.at[STEPS - 1 - i, h, 0], c2r.at[i, h])
         proj = pb[STEPS - 1 - i, h].reshape(hb, ranks)
+
+        def to_owner(d):
+            who = lax.rem(y + 1 + d, RANKS)
+            for part in range(2):
+                rs_s[i, h, d, part] = nt(proj, rows(u_v, 2 * who + part)).astype(BF16)
+            send(rs_s.at[i, h, d], rs_r.at[i, h, d], rss.at[i, h], rsr.at[i, h], (state, who))
+
+        each(0, RANKS - 1, to_owner)
+        pl.when(jnp.logical_and(i == 0, h == 0))(columns3)
         sums = nt(csm[...], proj)
         ms[i, h, 0:1, 0:hb] = sums[0:1] + sums[1:2] + sums[2:3]
         for d, who in enumerate((yp, yo, ym)):
             send(ms.at[i, h], mr.at[i, h, d], mss.at[i, h], msr.at[i, h], (state, who))
-        for part in range(2):
-            for d, who in ((1, yo), (0, yp), (2, ym)):
-                rs_s[i, h, part, d] = nt(proj, rows(u_v, 2 * who + part)).astype(BF16)
-                send(rs_s.at[i, h, part, d], rs_r.at[i, h, part, d], rss.at[i, h, part], rsr.at[i, h, part], (state, who))
+
+    def raw_own(i, h):
+        proj = pb[STEPS - 1 - i, h].reshape(hb, ranks)
         for part in range(2):
             keep[h, part] = nt(proj, rows(u_v, 2 * y + part))
 
@@ -240,62 +270,69 @@
         return mass.T[0:hb, 0:1] / states_all
 
     def own(i, h):
+        await_bytes(rs_r.at[i, h], rsr.at[i, h])
         mass = mass_of(i, h)
         for part in range(2):
-            await_bytes(rs_r.at[i, h, part], rsr.at[i, h, part])
             total = keep[h, part]
             for d in range(RANKS - 1):
-                total += rs_r[i, h, part, d].astype(F32)
+                total += rs_r[i, h, d, part].astype(F32)
             new = (total / mass).astype(BF16).astype(F32)
-            j = 2 * y + part
-            w[i + 1, h, j] = (emit[i, h, part] * new).astype(BF16)
-            for who in (yo, yp, ym):
-                send(w.at[i + 1, h, j], w.at[i + 1, h, j], ags.at[i, h, part], agr.at[i, h, part], (state, who))
-
-    def landed(i, h, part):
-        await_bytes(w.at[i + 1, h, pl.ds(0, RANKS - 1)], agr.at[i, h, part])
+            w[i + 1, h, 2 * y + part] = (emit[i, h, part] * new).astype(BF16)
+        shard = w.at[i + 1, h, pl.ds(2 * y, 2)]
+        for who in (yo, yp, ym):
+            send(shard, shard, ags.at[i, h], agr.at[i, h], (state, who))
+
+    def landed(i, h):
+        await_bytes(w.at[i + 1, h, pl.ds(0, 2 * (RANKS - 1))], agr.at[i, h])
 
     def project(i, h):
         def term(j):
             return nn(w[i, h, j], rows(v_v, j))
 
-        total = term(2 * y) + term(2 * y + 1)
-        for part in range(2):
-            landed(i - 1, h, part)
-            for who in (yp, yo, ym):
-                total += term(2 * who + part)
-        acc[h] = total
+        def shard(who):
+            return term(2 * who) + term(2 * who + 1)
+
+        total = shard(y)
+        landed(i - 1, h)
+        acc[h] = total + shard(yp) + shard(yo) + shard(ym)
         sum1(i, h)
 
     def turn(i):
         t = STEPS - 1 - i
 
         def one(j, carry):
-            both = jnp.concatenate([w[i, h, j] for h in range(HALVES)], axis=0)
+            both = jnp.concatenate([w[i, h, j] for h in range(CHAINS)], axis=0)
             wn[pl.ds(pl.multiple_of(j * blk, blk), blk), pl.ds(pl.multiple_of(t * batch, batch), batch)] = both.T
             return carry
 
         lax.fori_loop(0, BLOCKS, one, 0)
 
-    def gradients():
-        for i in range(STEPS):
-            await_bytes(fj.at[i, pl.ds(0, GROUP - 1)], f3r.at[i])
+    def grad_left():
         proj = pb[...].reshape(count, ranks)
-        fwd = fj[...].reshape(count, ranks)
 
         def one(j, carry):
             at = pl.ds(pl.multiple_of(j * blk, blk), blk)
             left_o[at, :] = (nn(fm_v[at, :], proj) / count).astype(BF16)
+            return carry
+
+        lax.fori_loop(0, BLOCKS, one, 0)
+
+    def grad_right():
+        for i in range(STEPS):
+            await_bytes(fj.at[i, pl.ds(0, GROUP - 1)], f3r.at[i])
+        fwd = fj[...].reshape(count, ranks)
+
+        def one(j, carry):
+            at = pl.ds(pl.multiple_of(j * blk, blk), blk)
             right_o[at, :] = (nn(wn[at, :], fwd) / count).astype(BF16)
             return carry
 
         lax.fori_loop(0, BLOCKS, one, 0)
 
-    a, b = 0, 1
-    sum1(0, a)
-    sum1(0, b)
-    columns2()
-    sum2(0, a)
+    each(0, CHAINS, lambda h: sum1(0, h))
+    u_l.wait()
+    columns1()
+    sum2(0, 0)
 
     ms[...] = jnp.zeros_like(ms)
     for t in range(STEPS - 1):
@@ -304,58 +341,46 @@
         for part in range(2):
             logits = nt(words[STEPS - 2 - i], rows(semb_v, 2 * y + part))
             em = jnp.exp(logits - ln_v[2 * y + part])
-            for h in range(HALVES):
+            for h in range(CHAINS):
                 emit[i, h, part] = em[h * hb:(h + 1) * hb]
     emit[STEPS - 1] = jnp.ones_like(emit[STEPS - 1])
-    columns3()
+    columns2()
+    sum2(0, 1)
     fm_l.wait()
-    fwd1(0)
-    sum2(0, b)
-    sum3(0, a)
-
-    def body(i, carry):
-        more = i < STEPS - 1
-        raw(i, a)
-
-        @pl.when(i > 0)
+    lax.fori_loop(0, CHAINS, lambda k, carry: (fwd1(0, k), carry)[1], 0)
+    sum3(0, 0)
+
+    def turn_of(n, carry):
+        i, k = n // CHAINS, n % CHAINS
+        raw(i, k)
+
+        @pl.when(n >= 1)
         def _():
-            sum2(i, b)
-
-        fwd2(i)
-        turn(i)
-
-        @pl.when(more)
+            own((n - 1) // CHAINS, (n - 1) % CHAINS)
+
+        i2, k2 = (n + 2) // CHAINS, (n + 2) % CHAINS
+        more = i2 < STEPS
+
+        @pl.when(jnp.logical_and(n >= 2, more))
         def _():
-            fwd1(i + 1)
-
-        own(i, a)
-        sum3(i, b)
-        raw(i, b)
-        fwd3(i)
-
-        @pl.when(more)
-        def _():
-            project(i + 1, a)
-            sum2(i + 1, a)
-
-        @pl.when(i == STEPS - 1)
-        def _():
-            gradients()
-
-        own(i, b)
-
-        @pl.when(more)
-        def _():
-            project(i + 1, b)
-            sum3(i + 1, a)
-
+            project(i2, k2)
+
+        pl.when(i < STEPS - 1)(lambda: fwd1(i + 1, k))
+        pl.when(more)(lambda: sum2(i2, k2))
+        pl.when(k == 0)(lambda: fwd2(i))
+        pl.when(k == 1)(lambda: fwd3(i))
+        pl.when(k == 2)(lambda: turn(i))
+        pl.when(n == CHAINS * STEPS - 1)(grad_right)
+        i3, k3 = (n + 1) // CHAINS, (n + 1) % CHAINS
+        pl.when(i3 < STEPS)(lambda: sum3(i3, k3))
+        raw_own(i, k)
         return carry
 
-    lax.fori_loop(0, STEPS, body, 0)
-
-    for h in range(HALVES):
-        for part in range(2):
-            landed(STEPS - 1, h, part)
+    lax.fori_loop(0, CHAINS * STEPS, turn_of, 0)
+    own(STEPS - 1, CHAINS - 1)
+    grad_left()
+
+    each(0, CHAINS, lambda h: landed(STEPS - 1, h))
     bt_o[...] = w[STEPS]
 
     for k in range(2):
@@ -365,14 +390,15 @@
         await_bytes(fr1.at[i], f1s.at[i])
         await_bytes(fr2.at[i, pl.ds(0, zs - 1)], f2s.at[i])
         await_bytes(fj.at[i, pl.ds(0, GROUP - 1)], f3s.at[i])
-        for h in range(HALVES):
+        def chain(h):
             await_bytes(cr.at[i, h], c1s.at[i, h])
             await_bytes(xb.at[i, h, pl.ds(0, chips - 1)], xs.at[i, h])
             await_bytes(pb.at[i, h, 0], c2s.at[i, h])
             await_bytes(mr.at[i, h], mss.at[i, h])
-            for part in range(2):
-                await_bytes(rs_r.at[i, h, part], rss.at[i, h, part])
-                await_bytes(w.at[i + 1, h, pl.ds(0, RANKS - 1)], ags.at[i, h, part])
+            await_bytes(rs_r.at[i, h], rss.at[i, h])
+            await_bytes(w.at[i + 1, h, pl.ds(0, 2 * (RANKS - 1))], ags.at[i, h])
+
+        each(0, CHAINS, chain)
         return carry
 
     lax.fori_loop(0, STEPS, left_all, 0)
@@ -385,7 +411,7 @@
     blk = bt.shape[3]
 
     def one(j, carry):
-        both = jnp.concatenate([bt[h, j] for h in range(HALVES)], axis=0)
+        both = jnp.concatenate([bt[h, j] for h in range(CHAINS)], axis=0)
         beta_v[pl.ds(pl.multiple_of(j * blk, blk), blk), :] = both.T
         return carry
 
@@ -405,7 +431,7 @@
     vocab = word_emb.shape[0]
     ranks = trans_left.shape[1]
     batch = beta_last.shape[1]
-    hb = batch // HALVES
+    hb = batch // CHAINS
     blk = local // BLOCKS
     dma = pltpu.SemaphoreType.DMA
     vm = pltpu.VMEM
@@ -413,25 +439,26 @@
         pltpu.SMEM((STEPS, batch), jnp.int32), vm((STEPS, batch), jnp.int32), vm((vocab // 16, 16, hidden), BF16),
         vm((local, hidden), BF16), vm((BLOCKS, 1, blk), F32), vm((local, batch), BF16), vm((local, STEPS * batch), BF16),
         vm((local, ranks), BF16), vm((local, ranks), BF16),
-        vm((batch, 16, hidden), BF16), vm((STEPS, batch, hidden), BF16), vm((STEPS + 1, HALVES, BLOCKS, hb, blk), BF16),
-        vm((local, STEPS * batch), BF16), vm((STEPS, HALVES, 2, hb, blk), F32), vm((HALVES, hb, ranks), F32),
-        vm((HALVES, 2, hb, blk), F32), vm((16, ranks), BF16), vm((STEPS, HALVES, 2, hb // 2, ranks), BF16),
-        vm((STEPS, HALVES, hb // 2, ranks), BF16), vm((STEPS, HALVES, hb // 2, ranks), BF16),
-        vm((STEPS, HALVES, chips, hb // 2, ranks), BF16),
+        vm((batch, 16, hidden), BF16), vm((STEPS, batch, hidden), BF16), vm((STEPS + 1, CHAINS, BLOCKS, hb, blk), BF16),
+        vm((local, STEPS * batch), BF16), vm((STEPS, CHAINS, 2, hb, blk), F32), vm((CHAINS, hb, ranks), F32),
+        vm((CHAINS, 2, hb, blk), F32), vm((16, ranks), BF16), vm((STEPS, CHAINS, 2, hb // 2, ranks), BF16),
+        vm((STEPS, CHAINS, hb // 2, ranks), BF16), vm((STEPS, CHAINS, hb // 2, ranks), BF16),
+        vm((STEPS, CHAINS, chips, hb // 2, ranks), BF16),
+        vm((batch, ranks), F32),
         vm((STEPS, GROUP, 16, ranks), BF16), vm((STEPS, GROUP - 1, 16, ranks), BF16),
         vm((STEPS, zs, 16, ranks), BF16), vm((STEPS, GROUP, 16, ranks), BF16),
         vm((2, 8, 128), F32), vm((GROUP - 1, 8, 128), F32), vm((zs - 1, 8, 128), F32),
-        vm((STEPS, HALVES, 2, RANKS - 1, hb, blk), BF16), vm((STEPS, HALVES, 2, RANKS - 1, hb, blk), BF16),
-        vm((STEPS, HALVES, 8, 128), F32), vm((STEPS, HALVES, RANKS - 1, 8, 128), F32),
-        dma((9,)),
-        *[dma((STEPS, HALVES)) for _ in range(6)], *[dma((STEPS,)) for _ in range(6)], dma((2,)), dma((2,)),
-        *[dma((STEPS, HALVES, 2)) for _ in range(4)], *[dma((STEPS, HALVES)) for _ in range(2)],
+        vm((STEPS, CHAINS, RANKS - 1, 2, hb, blk), BF16), vm((STEPS, CHAINS, RANKS - 1, 2, hb, blk), BF16),
+        vm((STEPS, CHAINS, 8, 128), F32), vm((STEPS, CHAINS, RANKS - 1, 8, 128), F32),
+        dma((8 + BLOCKS,)),
+        *[dma((STEPS, CHAINS)) for _ in range(6)], *[dma((STEPS,)) for _ in range(6)], dma((2,)), dma((2,)),
+        *[dma((STEPS, CHAINS)) for _ in range(6)],
     ]
     anywhere = pl.BlockSpec(memory_space=pl.ANY)
     inside = pl.BlockSpec(memory_space=pltpu.VMEM)
     left, right, bt = pl.pallas_call(
         functools.partial(recursion, states_all, zs),
-        out_shape=(vm((local, ranks), BF16), vm((local, ranks), BF16), vm((HALVES, BLOCKS, hb, blk), BF16)),
+        out_shape=(vm((local, ranks), BF16), vm((local, ranks), BF16), vm((CHAINS, BLOCKS, hb, blk), BF16)),
         in_specs=[anywhere] * 8,
         out_specs=[inside] * 3,
         scratch_shapes=scratch,

time: 120 us -> 104 us (0.87)
  Pallas kernels: 119 us -> 103 us
    pallas_call x1, Pallas kernels: 116 us -> 99.5 us  [on_device(): pl.pallas_call(functools.partial(recursion, states_all, zs), out_shape=(v...]
where the time goes in v3:
time: 104 us
  Pallas kernels  103 us (99%)
    pallas_call x1, Pallas kernels, on_device(): pl.pallas_call(functools.partial(recursion, states_all, zs), out_shape=(v...  99.5 us
    pallas_call x1, Pallas kernels, on_device(): pl.pallas_call(finish, out_shape=(jax.ShapeDtypeStruct((local, batch), BF...  3.64 us

profile of v3, /device:TPU:1, one launch (start us, length us, event | category | flops | bytes accessed | tf_op | source)
XLA Modules:
  0.0 103.8 jit_solution(2172191718184189786)
XLA Ops:
  0.6 99.5 %recursion.1 = (bf16[4096,512]{1,0:T(8,128)(2,1)S(1)}, bf16[4096,512]{1,0:T(8,128)(2,1)S(1)}, bf16[4,8,32,512]{3,2,1,0:T(8,128)(2,1)S(1)}) custom-call(s32[3,128]{1,0:T(4,128)} %ids.1, bf16[625,16,128]{2,1,0:T(8,128)(2,1)} %bitcast.2, bf16[4096,128]{1,0:T(8,128)(2,1)} %semb.1, f32[8,1,512]{2,1,0:T(1,128)} %bitcast.3, bf16[4096,128]{1,0:T(8,128)(2,1)} %beta.1, ...), custom_call_target="tpu_custom_call" | custom-call | tf_op jit(solution)/shard_map/recursion/pallas_call | solution.py:459
  100.1 3.6 %finish.1 = (bf16[4096,128]{1,0:T(8,128)(2,1)}, bf16[4096,512]{1,0:T(8,128)(2,1)}, bf16[4096,512]{1,0:T(8,128)(2,1)}) custom-call(bf16[4,8,32,512]{3,2,1,0:T(8,128)(2,1)S(1)} %get-tuple-element.6.bt, bf16[4096,512]{1,0:T(8,128)(2,1)S(1)} %get-tuple-element.7.left, bf16[4096,512]{1,0:T(8,128)(2,1)S(1)} %get-tuple-element.8.right), custom_call_target="tpu_custom_call" | custom-call | tf_op jit(solution)/shard_map/finish/pallas_call | solution.py:473

commit v4 on v3

--- a/solution.py
+++ b/solution.py
@@ -170,7 +170,7 @@
         v_l(j).wait()
         return total + nn(wt, rows(v_v, j))
 
-    total = lax.fori_loop(0, BLOCKS, first, jnp.zeros((batch, ranks), F32), unroll=2)
+    total = lax.fori_loop(0, BLOCKS, first, jnp.zeros((batch, ranks), F32), unroll=4)
     for h in range(CHAINS):
         acc[h] = total[h * hb:(h + 1) * hb]
 
@@ -246,13 +246,11 @@
         await_bytes(pb.at[STEPS - 1 - i, h, 0], c2r.at[i, h])
         proj = pb[STEPS - 1 - i, h].reshape(hb, ranks)
 
-        def to_owner(d):
-            who = lax.rem(y + 1 + d, RANKS)
+        for d, who in ((1, yo), (0, yp), (2, ym)):
             for part in range(2):
                 rs_s[i, h, d, part] = nt(proj, rows(u_v, 2 * who + part)).astype(BF16)
             send(rs_s.at[i, h, d], rs_r.at[i, h, d], rss.at[i, h], rsr.at[i, h], (state, who))
 
-        each(0, RANKS - 1, to_owner)
         pl.when(jnp.logical_and(i == 0, h == 0))(columns3)
         sums = nt(csm[...], proj)
         ms[i, h, 0:1, 0:hb] = sums[0:1] + sums[1:2] + sums[2:3]
@@ -352,39 +350,39 @@
 
     def turn_of(n, carry):
         i, k = n // CHAINS, n % CHAINS
+        i2, k2 = (n + 2) // CHAINS, (n + 2) % CHAINS
+        i3, k3 = (n + 1) // CHAINS, (n + 1) % CHAINS
+        more = i2 < STEPS
         raw(i, k)
+        pl.when(i < STEPS - 1)(lambda: fwd1(i + 1, k))
 
         @pl.when(n >= 1)
         def _():
             own((n - 1) // CHAINS, (n - 1) % CHAINS)
 
-        i2, k2 = (n + 2) // CHAINS, (n + 2) % CHAINS
-        more = i2 < STEPS
+        raw_own(i, k)
+        pl.when(k == 0)(lambda: fwd2(i))
+        pl.when(k == 1)(lambda: fwd3(i))
+        pl.when(k == 2)(lambda: turn(i))
 
         @pl.when(jnp.logical_and(n >= 2, more))
         def _():
             project(i2, k2)
 
-        pl.when(i < STEPS - 1)(lambda: fwd1(i + 1, k))
         pl.when(more)(lambda: sum2(i2, k2))
-        pl.when(k == 0)(lambda: fwd2(i))
-        pl.when(k == 1)(lambda: fwd3(i))
-        pl.when(k == 2)(lambda: turn(i))
+        pl.when(i3 < STEPS)(lambda: sum3(i3, k3))
         pl.when(n == CHAINS * STEPS - 1)(grad_right)
-        i3, k3 = (n + 1) // CHAINS, (n + 1) % CHAINS
-        pl.when(i3 < STEPS)(lambda: sum3(i3, k3))
-        raw_own(i, k)
         return carry
 
     lax.fori_loop(0, CHAINS * STEPS, turn_of, 0)
     own(STEPS - 1, CHAINS - 1)
     grad_left()
 
-    each(0, CHAINS, lambda h: landed(STEPS - 1, h))
-    bt_o[...] = w[STEPS]
-
     for k in range(2):
         await_bytes((cr1, cr2)[k], cs_s.at[k])
+
+    def shard_left(i, h):
+        await_bytes(w.at[i + 1, h, pl.ds(0, 2 * (RANKS - 1))], ags.at[i, h])
 
     def left_all(i, carry):
         await_bytes(fr1.at[i], f1s.at[i])
@@ -396,12 +394,17 @@
             await_bytes(pb.at[i, h, 0], c2s.at[i, h])
             await_bytes(mr.at[i, h], mss.at[i, h])
             await_bytes(rs_r.at[i, h], rss.at[i, h])
-            await_bytes(w.at[i + 1, h, pl.ds(0, 2 * (RANKS - 1))], ags.at[i, h])
+            pl.when(jnp.logical_or(i < STEPS - 1, h < CHAINS - 1))(lambda: shard_left(i, h))
 
         each(0, CHAINS, chain)
         return carry
 
     lax.fori_loop(0, STEPS, left_all, 0)
+
+    for h in range(CHAINS):
+        landed(STEPS - 1, h)
+        bt_o[h] = w[STEPS, h]
+    shard_left(STEPS - 1, CHAINS - 1)
 
 
 def finish(bt, left, right, beta_o, left_o, right_o, beta_v, sems):

time: 104 us -> 101 us (0.971)
  Pallas kernels: 103 us -> 99.8 us
    pallas_call x1, Pallas kernels: 99.5 us -> 96.2 us  [on_device(): pl.pallas_call(functools.partial(recursion, states_all, zs), out_shape=(v...]
where the time goes in v4:
time: 101 us; the launch traced here: 100 us
  Pallas kernels  99.8 us (99%)
    pallas_call x1, Pallas kernels, on_device(): pl.pallas_call(functools.partial(recursion, states_all, zs), out_shape=(v...  96.2 us
    pallas_call x1, Pallas kernels, on_device(): pl.pallas_call(finish, out_shape=(jax.ShapeDtypeStruct((local, batch), BF...  3.64 us

profile of v4, /device:TPU:1, one launch (start us, length us, event | category | flops | bytes accessed | tf_op | source)
XLA Modules:
  0.0 100.5 jit_solution(8706394964429892648)
XLA Ops:
  0.6 96.2 %recursion.1 = (bf16[4096,512]{1,0:T(8,128)(2,1)S(1)}, bf16[4096,512]{1,0:T(8,128)(2,1)S(1)}, bf16[4,8,32,512]{3,2,1,0:T(8,128)(2,1)S(1)}) custom-call(s32[3,128]{1,0:T(4,128)} %ids.1, bf16[625,16,128]{2,1,0:T(8,128)(2,1)} %bitcast.2, bf16[4096,128]{1,0:T(8,128)(2,1)} %semb.1, f32[8,1,512]{2,1,0:T(1,128)} %bitcast.3, bf16[4096,128]{1,0:T(8,128)(2,1)} %beta.1, ...), custom_call_target="tpu_custom_call" | custom-call | tf_op jit(solution)/shard_map/recursion/pallas_call | solution.py:462
  96.8 3.6 %finish.1 = (bf16[4096,128]{1,0:T(8,128)(2,1)}, bf16[4096,512]{1,0:T(8,128)(2,1)}, bf16[4096,512]{1,0:T(8,128)(2,1)}) custom-call(bf16[4,8,32,512]{3,2,1,0:T(8,128)(2,1)S(1)} %get-tuple-element.6.bt, bf16[4096,512]{1,0:T(8,128)(2,1)S(1)} %get-tuple-element.7.left, bf16[4096,512]{1,0:T(8,128)(2,1)S(1)} %get-tuple-element.8.right), custom_call_target="tpu_custom_call" | custom-call | tf_op jit(solution)/shard_map/finish/pallas_call | solution.py:476

commit v5 on v4

--- a/solution.py
+++ b/solution.py
@@ -170,7 +170,7 @@
         v_l(j).wait()
         return total + nn(wt, rows(v_v, j))
 
-    total = lax.fori_loop(0, BLOCKS, first, jnp.zeros((batch, ranks), F32), unroll=4)
+    total = lax.fori_loop(0, BLOCKS, first, jnp.zeros((batch, ranks), F32), unroll=8)
     for h in range(CHAINS):
         acc[h] = total[h * hb:(h + 1) * hb]
 
@@ -325,7 +325,7 @@
             right_o[at, :] = (nn(wn[at, :], fwd) / count).astype(BF16)
             return carry
 
-        lax.fori_loop(0, BLOCKS, one, 0)
+        lax.fori_loop(0, BLOCKS, one, 0, unroll=2)
 
     each(0, CHAINS, lambda h: sum1(0, h))
     u_l.wait()

time: 101 us -> 101 us (level)
  no operation moved by 1% of the time
where the time goes in v5:
time: 101 us
  Pallas kernels  99.9 us (99%)
    pallas_call x1, Pallas kernels, on_device(): pl.pallas_call(functools.partial(recursion, states_all, zs), out_shape=(v...  96.2 us
    pallas_call x1, Pallas kernels, on_device(): pl.pallas_call(finish, out_shape=(jax.ShapeDtypeStruct((local, batch), BF...  3.64 us

profile of v5, /device:TPU:1, one launch (start us, length us, event | category | flops | bytes accessed | tf_op | source)
XLA Modules:
  0.0 100.5 jit_solution(9107084258024408261)
XLA Ops:
  0.6 96.2 %recursion.1 = (bf16[4096,512]{1,0:T(8,128)(2,1)S(1)}, bf16[4096,512]{1,0:T(8,128)(2,1)S(1)}, bf16[4,8,32,512]{3,2,1,0:T(8,128)(2,1)S(1)}) custom-call(s32[3,128]{1,0:T(4,128)} %ids.1, bf16[625,16,128]{2,1,0:T(8,128)(2,1)} %bitcast.2, bf16[4096,128]{1,0:T(8,128)(2,1)} %semb.1, f32[8,1,512]{2,1,0:T(1,128)} %bitcast.3, bf16[4096,128]{1,0:T(8,128)(2,1)} %beta.1, ...), custom_call_target="tpu_custom_call" | custom-call | tf_op jit(solution)/shard_map/recursion/pallas_call | solution.py:462
  96.9 3.6 %finish.1 = (bf16[4096,128]{1,0:T(8,128)(2,1)}, bf16[4096,512]{1,0:T(8,128)(2,1)}, bf16[4096,512]{1,0:T(8,128)(2,1)}) custom-call(bf16[4,8,32,512]{3,2,1,0:T(8,128)(2,1)S(1)} %get-tuple-element.6.bt, bf16[4096,512]{1,0:T(8,128)(2,1)S(1)} %get-tuple-element.7.left, bf16[4096,512]{1,0:T(8,128)(2,1)S(1)} %get-tuple-element.8.right), custom_call_target="tpu_custom_call" | custom-call | tf_op jit(solution)/shard_map/finish/pallas_call | solution.py:476
